TPU v7x, 256 devices: a whole 4x4x8 slice. The times are simulated.
256 devices in a mesh: subj: 4 (over z_hi, core), slab: 64 (over z_lo, y, x).
Axes of the slice: x: 4, y: 4, z: 8 (z_hi: 2, z_lo: 4; z = z_hi * 4 + z_lo), core: 2. Of those that a mesh axis runs over, the one named last changes fastest.
Arguments:
- image: bfloat16 [4, 20, 64, 2, 320], P('subj', None, 'slab'), may hold values from -6 to 6
- upstream: float32 [4, 20, 64, 2, 320], P('subj', None, 'slab'), may hold values from -6 to 6
- coil_maps: float32 [4, 2, 8, 64, 2, 320], P('subj', None, None, 'slab'), may hold values from -1.5 to 1.5
- kernel: float32 [10, 10, 64, 2, 320], P(None, None, None, None, 'slab'), may hold values from -0.5 to 5.5, as said below
- w_first: bfloat16 [3, 3, 3, 64, 20], replicated, may hold values from -0.25 to 0.25
- w_second: bfloat16 [3, 3, 3, 64, 64], replicated, may hold values from -0.15625 to 0.15625
- w_third: bfloat16 [3, 3, 3, 64, 64], replicated, may hold values from -0.15625 to 0.15625
- w_fourth: bfloat16 [3, 3, 3, 64, 64], replicated, may hold values from -0.15625 to 0.15625
- w_last: bfloat16 [3, 3, 3, 20, 64], replicated, may hold values from -0.15625 to 0.15625
Outputs:
- image_grad: float32 [4, 20, 64, 2, 320], P('subj', None, 'slab')
- w_first_grad: float32 [3, 3, 3, 64, 20], replicated
- w_second_grad: float32 [3, 3, 3, 64, 64], replicated
- w_third_grad: float32 [3, 3, 3, 64, 64], replicated
- w_fourth_grad: float32 [3, 3, 3, 64, 64], replicated
- w_last_grad: float32 [3, 3, 3, 20, 64], replicated
Inputs may be any that keep to these rules, and one draw needn't show every extreme that they name: kernel[:, :, kz, x, ky] is a symmetric positive definite 10 x 10 matrix at every k-space point.
All inputs are finite; a program needn't handle non-finite values.
Results may differ from a plain program's by a relative error of at most 0.014.
Values may be sent and summed in bfloat16 or wider, within the bound.
A program may use at most 128 MiB of HBM per device.

v0:
```python
import math
import jax
import jax.numpy as jnp
from jax import lax
from jax.sharding import PartitionSpec as P

ETA_STEP = 0.5
PRECISE = lax.Precision.HIGHEST


def padded_2(block, sides, width):
    for axis, dim in sides:
        count = lax.axis_size(axis)
        forward = [(i, i + 1) for i in range(count - 1)]
        backward = [(target, source) for source, target in forward]
        low = lax.ppermute(
            lax.slice_in_dim(block, block.shape[dim] - width, None, axis=dim), axis, forward
        )
        high = lax.ppermute(lax.slice_in_dim(block, 0, width, axis=dim), axis, backward)
        block = jnp.concatenate([low, block, high], axis=dim)
    return block


def silu_slope(pre_act):
    sigmoid = jax.nn.sigmoid(pre_act)
    return sigmoid * (1.0 + pre_act * (1.0 - sigmoid))


def offsets():
    return [(off_z, off_x, off_y) for off_z in range(3) for off_x in range(3) for off_y in range(3)]


def tap_set(padded_z, forward):
    padded = jnp.pad(padded_z, ((0, 0), (0, 0), (1, 1), (1, 1)))
    count_z = padded_z.shape[1] - 2
    count_x = padded_z.shape[2]
    count_y = padded_z.shape[3]
    pieces = []
    for off_z, off_x, off_y in offsets():
        if forward:
            start_z, start_x, start_y = (off_z, off_x, off_y)
        else:
            start_z, start_x, start_y = (2 - off_z, 2 - off_x, 2 - off_y)
        pieces.append(
            padded[
                :,
                start_z : start_z + count_z,
                start_x : start_x + count_x,
                start_y : start_y + count_y,
            ]
        )
    return jnp.stack(pieces)


def planes_in(activation):
    return padded_2(activation, (("slab", 1),), 1)


def planes_back(delta_grad):
    return padded_2(delta_grad, (("slab", 1),), 1)


def dft_tables(length):
    positions = jnp.arange(length, dtype=jnp.int32)
    products = positions[:, None] * positions[None, :] % length
    angles = products.astype(jnp.float32) * (2.0 * math.pi / length)
    scaling = 1.0 / math.sqrt(length)
    return (jnp.cos(angles) * scaling, jnp.sin(angles) * scaling)


def transform(real_part, imag_part, cosine, sine, pattern, inverse):
    real_cos = jnp.einsum(pattern, real_part, cosine, precision=PRECISE)
    real_sin = jnp.einsum(pattern, real_part, sine, precision=PRECISE)
    imag_cos = jnp.einsum(pattern, imag_part, cosine, precision=PRECISE)
    imag_sin = jnp.einsum(pattern, imag_part, sine, precision=PRECISE)
    if inverse:
        return (real_cos - imag_sin, imag_cos + real_sin)
    return (real_cos + imag_sin, imag_cos - real_sin)


def kspace_mix(arrived, kernel_band, cosine_depth, sine_depth):
    depth_real, depth_imag = transform(
        arrived[0], arrived[1], cosine_depth, sine_depth, "crxyz,zk->crxyk", False
    )
    mixed_real = jnp.einsum("rsxyk,csxyk->crxyk", kernel_band, depth_real, precision=PRECISE)
    mixed_imag = jnp.einsum("rsxyk,csxyk->crxyk", kernel_band, depth_imag, precision=PRECISE)
    back_real, back_imag = transform(
        mixed_real, mixed_imag, cosine_depth, sine_depth, "crxyz,zk->crxyk", True
    )
    return jnp.stack((back_real, back_imag))


def normal_operator(field, maps, kernel_band, tables):
    cosine_rows, sine_rows, cosine_depth, sine_depth = tables
    components = field.shape[0] // 2
    vec_real = field[:components][None]
    vec_imag = field[components:][None]
    map_real = maps[0][:, None]
    map_imag = maps[1][:, None]
    coil_real = map_real * vec_real - map_imag * vec_imag
    coil_imag = map_real * vec_imag + map_imag * vec_real
    spec_real, spec_imag = transform(
        coil_real, coil_imag, cosine_rows, sine_rows, "crzxn,nk->crxkz", False
    )
    spectra = jnp.stack((spec_real, spec_imag))
    arrived = lax.all_to_all(spectra, "slab", split_axis=4, concat_axis=5, tiled=True)
    mixed = kspace_mix(arrived, kernel_band, cosine_depth, sine_depth)
    returned = lax.all_to_all(mixed, "slab", split_axis=5, concat_axis=4, tiled=True)
    back_real, back_imag = transform(
        returned[0], returned[1], cosine_rows, sine_rows, "crxnz,nk->crzxk", True
    )
    out_real = jnp.sum(map_real * back_real + map_imag * back_imag, axis=0)
    out_imag = jnp.sum(map_real * back_imag - map_imag * back_real, axis=0)
    return jnp.concatenate((out_real, out_imag), axis=0)


def body(image, upstream, coil_maps, kernel, w_first, w_second, w_third, w_fourth, w_last):
    weights = (w_first, w_second, w_third, w_fourth, w_last)
    weight_taps = [weight.reshape(27, weight.shape[3], weight.shape[4]) for weight in weights]
    cosine_rows, sine_rows = dft_tables(image.shape[4])
    cosine_depth, sine_depth = dft_tables(kernel.shape[2])
    tables = (cosine_rows, sine_rows, cosine_depth, sine_depth)
    kernel_band = jnp.transpose(kernel, (0, 1, 3, 4, 2))
    local_sums = [jnp.zeros(taps.shape, jnp.float32) for taps in weight_taps]
    direct = upstream[0] - ETA_STEP * normal_operator(
        upstream[0], coil_maps[0], kernel_band, tables
    )
    activation = image[0]
    tap_sets = []
    pre_acts = []
    for level in range(5):
        inputs = tap_set(planes_in(activation), True)
        tap_sets.append(inputs)
        if level < 4:
            pre_act = jnp.einsum(
                "toi,tizxy->ozxy", weight_taps[level], inputs, preferred_element_type=jnp.float32
            )
            pre_acts.append(pre_act)
            activation = jax.nn.silu(pre_act).astype(jnp.bfloat16)
    delta_grad = direct.astype(jnp.bfloat16)
    back_grad = direct
    for level in (4, 3, 2, 1, 0):
        local_sums[level] = jnp.einsum(
            "ozxy,tizxy->toi", delta_grad, tap_sets[level], preferred_element_type=jnp.float32
        )
        shifted = tap_set(planes_back(delta_grad), False)
        back_grad = jnp.einsum(
            "toi,tozxy->izxy", weight_taps[level], shifted, preferred_element_type=jnp.float32
        )
        if level > 0:
            delta_grad = (back_grad * silu_slope(pre_acts[level - 1])).astype(jnp.bfloat16)
    image_grads = [direct + back_grad]
    local_tuple = (local_sums[0], local_sums[1], local_sums[2], local_sums[3], local_sums[4])
    summed = lax.psum(
        (local_tuple[0], local_tuple[1], local_tuple[2], local_tuple[3], local_tuple[4]),
        ("subj", "slab"),
    )
    total_cells = (
        image.shape[0]
        * lax.axis_size("subj")
        * image.shape[2]
        * lax.axis_size("slab")
        * image.shape[3]
        * image.shape[4]
    )
    scaling = 1.0 / math.sqrt(total_cells)
    results = [summed[level].reshape(weights[level].shape) * scaling for level in range(5)]
    return (jnp.stack(image_grads), results[0], results[1], results[2], results[3], results[4])


def solution(mesh):
    in_specs = (
        P("subj", None, "slab", None, None),
        P("subj", None, "slab", None, None),
        P("subj", None, None, "slab", None, None),
        P(None, None, None, None, "slab"),
        P(),
        P(),
        P(),
        P(),
        P(),
    )
    out_specs = (P("subj", None, "slab", None, None), P(), P(), P(), P(), P())
    return jax.shard_map(body, mesh=mesh, in_specs=in_specs, out_specs=out_specs, check_vma=False)
```

profile of v0, /device:TPU:4, one launch (start us, length us, event | category | flops | bytes accessed | tf_op | source)
XLA Modules:
  0.0 623.4 jit_solution(8635704941181876310)
XLA Ops:
  9.8 3.4 collective-permute-start.2
  24.2 4.4 collective-permute-start.4
  34.4 3.1 collective-permute-start.7
  37.5 5.0 collective-permute-start.6
  50.2 6.0 collective-permute-start.8
  65.4 6.2 %collective-permute-start.18 = (bf16[64,1,2,320]{3,0,2,1:T(8,128)(2,1)S(1)}, bf16[64,1,2,320]{3,0,2,1:T(8,128)(2,1)S(1)}, u32[]{:S(2)}, u32[]{:S(2)}) collective-permute-start(bf16[64,1,2,320]{3,0,2,1:T(8,128)(2,1)S(1)} %fusion.346), channel_id=1, source_target_pairs={{0,1},{1,2},{2,3},{3,4},{4,5},{5,6},{6,7},{7,8},{8,9},{9,10},{10,1... | collective-permute-start | bytes 245768 | tf_op jit(solution)/shard_map/ppermute | solution.py:16
  71.7 5.0 copy.3471
  76.6 8.8 %reshape.355 = f32[64,1,1600]{2,1,0:T(1,128)} reshape(f32[320,2,1,8,2,10]{5,4,3,2,1,0:T(2,128)} %bitcast.1345) | data formatting | bytes 819200
  85.4 23.7 %all-to-all-start = ((f32[64,1,1600]{2,1,0:T(1,128)}), f32[64,1,1600]{2,1,0:T(1,128)S(1)}, u32[]{:S(2)}, u32[]{:S(2)}) async-start(f32[64,1,1600]{2,1,0:T(1,128)} %reshape.355), calls=%async_computation | async-start | bytes 851968 | tf_op jit(solution)/shard_map/all_to_all | solution.py:106
  109.2 4.2 copy.3476
  131.0 9.9 %reshape.356 = f32[320,2,1,8,2,10]{5,4,3,2,1,0:T(2,128)} reshape(f32[64,1600]{1,0:T(8,128)S(1)} %reduce.2) | data formatting | bytes 819200
  140.9 2.8 copy.3472
  156.2 3.1 copy.3478
  159.2 12.0 %convolution_bitcast_fusion = f32[8,10,2,5,64]{1,0,4,3,2:T(8,128)} fusion(f32[8,10,2,5,64]{1,0,4,3,2:T(8,128)} %copy.3478, f32[10,10,2,5,64]{1,0,4,3,2:T(8,128)} %copy.3476), kind=kOutput, calls=%fused_computation.26 | convolution fusion | flops 6144000 | bytes 665600 | tf_op jit(solution)/shard_map/rsxyk,csxyk->crxyk/dot_general | solution.py:86
  176.8 3.1 copy.3475
  179.8 11.6 %convolution_bitcast_fusion.1 = f32[8,10,2,5,64]{1,0,4,3,2:T(8,128)} fusion(f32[8,10,2,5,64]{1,0,4,3,2:T(8,128)} %copy.3475, f32[10,10,2,5,64]{1,0,4,3,2:T(8,128)} %copy.3476), kind=kOutput, calls=%fused_computation.27 | convolution fusion | flops 6144000 | bytes 665600 | tf_op jit(solution)/shard_map/rsxyk,csxyk->crxyk/dot_general | solution.py:85
  196.5 5.9 copy.3483
  202.4 6.7 %reshape.357 = f32[64,1,1600]{2,1,0:T(1,128)} reshape(f32[64,2,2,5,8,10]{5,4,3,2,1,0:T(8,128)} %bitcast.1347) | data formatting | bytes 819200
  209.2 10.7 %all-to-all-start.1 = ((f32[64,1,1600]{2,1,0:T(1,128)}), f32[64,1,1600]{2,1,0:T(1,128)S(1)}, u32[]{:S(2)}, u32[]{:S(2)}) async-start(f32[64,1,1600]{2,1,0:T(1,128)} %reshape.357), calls=%async_computation.1 | async-start | bytes 851968 | tf_op jit(solution)/shard_map/all_to_all | solution.py:108
  222.7 8.3 %all-to-all-done.1 = f32[64,1,1600]{2,1,0:T(1,128)S(1)} async-done(((f32[64,1,1600]{2,1,0:T(1,128)}), f32[64,1,1600]{2,1,0:T(1,128)S(1)}, u32[]{:S(2)}, u32[]{:S(2)}) %all-to-all-start.1) | async-done | bytes 409632 | tf_op jit(solution)/shard_map/all_to_all | solution.py:108
  232.7 7.4 %reshape.358 = f32[64,2,2,5,8,10]{5,4,3,2,1,0:T(8,128)} reshape(f32[64,1600]{1,0:T(8,128)S(1)} %reduce.3) | data formatting | bytes 819200
  240.1 2.8 bitcast_bitcast_fusion
  251.9 3.4 copy.3486
  263.7 3.3 add_reduce_fusion
  267.0 3.5 collective-permute-start.1
  278.3 3.4 collective-permute-start.11
  285.9 3.6 fusion.37
  292.3 3.4 collective-permute-start.13
  295.7 4.4 collective-permute-start.12
  307.1 6.2 collective-permute-start.14
  320.0 6.4 %collective-permute-start.16 = (bf16[64,1,2,320]{3,0,2,1:T(8,128)(2,1)S(1)}, bf16[64,1,2,320]{3,0,2,1:T(8,128)(2,1)S(1)}, u32[]{:S(2)}, u32[]{:S(2)}) collective-permute-start(bf16[64,1,2,320]{3,0,2,1:T(8,128)(2,1)S(1)} %bitcast.1354), channel_id=1, source_target_pairs={{0,1},{1,2},{2,3},{3,4},{4,5},{5,6},{6,7},{7,8},{8,9},{9,10},{10,1... | collective-permute-start | bytes 245768 | tf_op jit(solution)/shard_map/ppermute | solution.py:16
  332.0 275.3 %all-reduce.13.cloned.1.call-done = (f32[27,64,20]{1,0,2:T(8,128)}, f32[27,64,64]{1,2,0:T(8,128)}, f32[27,64,64]{1,2,0:T(8,128)}, f32[27,64,64]{1,2,0:T(8,128)}, f32[27,20,64]{2,1,0:T(8,128)}) async-done(((f32[27,64,20]{1,0,2:T(8,128)}, f32[27,64,64]{1,2,0:T(8,128)}, f32[27,64,64]{1,2,0:T(8,128)}, f32[27,64,64]{1,2,0:T(8,128)}, f32[27,20,64]{2,1,0:T(8,128)}), (f32[27,64,20]{1,0,2:T(8,128)}, ...) | async-done | bytes 1603600 | tf_op jit(solution)/shard_map/psum | solution.py:154
  (427 shorter events, 139.7 us)
Async XLA Ops:
  7.2 54.1 %copy-start = (bf16[3,3,3,64,64]{4,3,2,1,0:T(8,128)(2,1)S(1)}, bf16[3,3,3,64,64]{4,3,2,1,0:T(8,128)(2,1)}, u32[]{:S(2)}) copy-start(bf16[3,3,3,64,64]{4,3,2,1,0:T(8,128)(2,1)} %param.16) | copy-start | bytes 663556
  7.2 12.6 %copy-start.24 = (bf16[1,20,1,2,320]{4,3,2,1,0:T(2,128)(2,1)S(1)}, bf16[1,20,1,2,320]{4,3,2,1,0:T(2,128)(2,1)}, u32[]{:S(2)}) copy-start(bf16[1,20,1,2,320]{4,3,2,1,0:T(2,128)(2,1)} %param.9) | copy-start | bytes 76804
  7.2 13.9 %copy-start.22 = (bf16[3,3,3,64,20]{3,4,2,1,0:T(8,128)(2,1)S(1)}, bf16[3,3,3,64,20]{3,4,2,1,0:T(8,128)(2,1)}, u32[]{:S(2)}) copy-start(bf16[3,3,3,64,20]{3,4,2,1,0:T(8,128)(2,1)} %param.13) | copy-start | bytes 207364
  7.2 10.4 %collective-permute-start.3 = (bf16[20,1,2,320]{3,2,0,1:T(2,128)(2,1)}, bf16[20,1,2,320]{3,2,0,1:T(2,128)(2,1)S(1)}, u32[]{:S(2)}, u32[]{:S(2)}) collective-permute-start(bf16[20,1,2,320]{3,2,0,1:T(2,128)(2,1)} %bitcast.1381), channel_id=1, source_target_pairs={{1,0},{2,1},{3,2},{4,3},{5,4},{6,5},{7,6},{8,7},{9,8},{10,9},{11,1... | collective-permute-start | bytes 76808 | tf_op jit(solution)/shard_map/ppermute | solution.py:19
  9.8 7.8 %collective-permute-start.2 = (bf16[20,1,2,320]{3,2,0,1:T(2,128)(2,1)}, bf16[20,1,2,320]{3,2,0,1:T(2,128)(2,1)S(1)}, u32[]{:S(2)}, u32[]{:S(2)}) collective-permute-start(bf16[20,1,2,320]{3,2,0,1:T(2,128)(2,1)} %bitcast.1382), channel_id=1, source_target_pairs={{0,1},{1,2},{2,3},{3,4},{4,5},{5,6},{6,7},{7,8},{8,9},{9,10},{10,1... | collective-permute-start | bytes 76808 | tf_op jit(solution)/shard_map/ppermute | solution.py:16
  21.4 11.2 %copy-start.14 = (f32[64,2,320]{2,0,1:T(8,128)}, f32[64,2,320]{2,0,1:T(8,128)S(1)}, u32[]{:S(2)}) copy-start(f32[64,2,320]{2,0,1:T(8,128)S(1)} %convolution_bitcast_fusion.3) | copy-start | bytes 491524
  21.5 10.0 %collective-permute-start.5 = (bf16[64,1,2,320]{3,0,2,1:T(8,128)(2,1)S(1)}, bf16[64,1,2,320]{3,0,2,1:T(8,128)(2,1)S(1)}, u32[]{:S(2)}, u32[]{:S(2)}) collective-permute-start(bf16[64,1,2,320]{3,0,2,1:T(8,128)(2,1)S(1)} %fusion.343), channel_id=1, source_target_pairs={{1,0},{2,1},{3,2},{4,3},{5,4},{6,5},{7,6},{8,7},{9,8},{10,9},{11,1... | collective-permute-start | bytes 245768 | tf_op jit(solution)/shard_map/ppermute | solution.py:19
  24.2 7.3 %collective-permute-start.4 = (bf16[64,1,2,320]{3,0,2,1:T(8,128)(2,1)S(1)}, bf16[64,1,2,320]{3,0,2,1:T(8,128)(2,1)S(1)}, u32[]{:S(2)}, u32[]{:S(2)}) collective-permute-start(bf16[64,1,2,320]{3,0,2,1:T(8,128)(2,1)S(1)} %fusion.343), channel_id=1, source_target_pairs={{0,1},{1,2},{2,3},{3,4},{4,5},{5,6},{6,7},{7,8},{8,9},{9,10},{10,1... | collective-permute-start | bytes 245768 | tf_op jit(solution)/shard_map/ppermute | solution.py:16
  33.7 11.6 %copy-start.1 = (bf16[27,64,1,2,320]{4,1,3,2,0:T(8,128)(2,1)}, bf16[27,64,1,2,320]{4,1,3,2,0:T(8,128)(2,1)S(1)}, u32[]{:S(2)}) copy-start(bf16[27,64,1,2,320]{4,1,3,2,0:T(8,128)(2,1)S(1)} %constant_dynamic-update-slice_fusion.54) | copy-start | bytes 6635524
  34.4 11.0 %collective-permute-start.7 = (bf16[64,1,2,320]{3,0,2,1:T(8,128)(2,1)S(1)}, bf16[64,1,2,320]{3,0,2,1:T(8,128)(2,1)S(1)}, u32[]{:S(2)}, u32[]{:S(2)}) collective-permute-start(bf16[64,1,2,320]{3,0,2,1:T(8,128)(2,1)S(1)} %fusion.344), channel_id=1, source_target_pairs={{1,0},{2,1},{3,2},{4,3},{5,4},{6,5},{7,6},{8,7},{9,8},{10,9},{11,1... | collective-permute-start | bytes 245768 | tf_op jit(solution)/shard_map/ppermute | solution.py:19
  37.5 7.8 %collective-permute-start.6 = (bf16[64,1,2,320]{3,0,2,1:T(8,128)(2,1)S(1)}, bf16[64,1,2,320]{3,0,2,1:T(8,128)(2,1)S(1)}, u32[]{:S(2)}, u32[]{:S(2)}) collective-permute-start(bf16[64,1,2,320]{3,0,2,1:T(8,128)(2,1)S(1)} %fusion.344), channel_id=1, source_target_pairs={{0,1},{1,2},{2,3},{3,4},{4,5},{5,6},{6,7},{7,8},{8,9},{9,10},{10,1... | collective-permute-start | bytes 245768 | tf_op jit(solution)/shard_map/ppermute | solution.py:16
  47.6 11.5 %copy-start.3 = (bf16[27,64,1,2,320]{4,1,3,2,0:T(8,128)(2,1)}, bf16[27,64,1,2,320]{4,1,3,2,0:T(8,128)(2,1)S(1)}, u32[]{:S(2)}) copy-start(bf16[27,64,1,2,320]{4,1,3,2,0:T(8,128)(2,1)S(1)} %constant_dynamic-update-slice_fusion.81) | copy-start | bytes 6635524
  48.3 10.8 %collective-permute-start.9 = (bf16[64,1,2,320]{3,0,2,1:T(8,128)(2,1)S(1)}, bf16[64,1,2,320]{3,0,2,1:T(8,128)(2,1)S(1)}, u32[]{:S(2)}, u32[]{:S(2)}) collective-permute-start(bf16[64,1,2,320]{3,0,2,1:T(8,128)(2,1)S(1)} %fusion.345), channel_id=1, source_target_pairs={{1,0},{2,1},{3,2},{4,3},{5,4},{6,5},{7,6},{8,7},{9,8},{10,9},{11,1... | collective-permute-start | bytes 245768 | tf_op jit(solution)/shard_map/ppermute | solution.py:19
  50.2 8.9 %collective-permute-start.8 = (bf16[64,1,2,320]{3,0,2,1:T(8,128)(2,1)S(1)}, bf16[64,1,2,320]{3,0,2,1:T(8,128)(2,1)S(1)}, u32[]{:S(2)}, u32[]{:S(2)}) collective-permute-start(bf16[64,1,2,320]{3,0,2,1:T(8,128)(2,1)S(1)} %fusion.345), channel_id=1, source_target_pairs={{0,1},{1,2},{2,3},{3,4},{4,5},{5,6},{6,7},{7,8},{8,9},{9,10},{10,1... | collective-permute-start | bytes 245768 | tf_op jit(solution)/shard_map/ppermute | solution.py:16
  63.4 59.1 %copy-start.8 = (f32[64,2,320]{2,0,1:T(8,128)}, f32[64,2,320]{2,0,1:T(8,128)S(1)}, u32[]{:S(2)}) copy-start(f32[64,2,320]{2,0,1:T(8,128)S(1)} %fusion.49) | copy-start | bytes 491524
  63.4 49.9 %collective-permute-start.19 = (bf16[64,1,2,320]{3,0,2,1:T(8,128)(2,1)S(1)}, bf16[64,1,2,320]{3,0,2,1:T(8,128)(2,1)S(1)}, u32[]{:S(2)}, u32[]{:S(2)}) collective-permute-start(bf16[64,1,2,320]{3,0,2,1:T(8,128)(2,1)S(1)} %fusion.346), channel_id=1, source_target_pairs={{1,0},{2,1},{3,2},{4,3},{5,4},{6,5},{7,6},{8,7},{9,8},{10,9},{11,1... | collective-permute-start | bytes 245768 | tf_op jit(solution)/shard_map/ppermute | solution.py:19
  65.4 48.0 %collective-permute-start.18 = (bf16[64,1,2,320]{3,0,2,1:T(8,128)(2,1)S(1)}, bf16[64,1,2,320]{3,0,2,1:T(8,128)(2,1)S(1)}, u32[]{:S(2)}, u32[]{:S(2)}) collective-permute-start(bf16[64,1,2,320]{3,0,2,1:T(8,128)(2,1)S(1)} %fusion.346), channel_id=1, source_target_pairs={{0,1},{1,2},{2,3},{3,4},{4,5},{5,6},{6,7},{7,8},{8,9},{9,10},{10,1... | collective-permute-start | bytes 245768 | tf_op jit(solution)/shard_map/ppermute | solution.py:16
  76.6 32.5 %copy-start.16 = (f32[10,10,64,2,5]{2,3,4,1,0:T(2,128)S(1)}, f32[10,10,64,2,5]{2,3,4,1,0:T(2,128)}, u32[]{:S(2)}) copy-start(f32[10,10,64,2,5]{2,3,4,1,0:T(2,128)} %param.12) | copy-start | bytes 768004
  85.4 43.4 %all-to-all-start = ((f32[64,1,1600]{2,1,0:T(1,128)}), f32[64,1,1600]{2,1,0:T(1,128)S(1)}, u32[]{:S(2)}, u32[]{:S(2)}) async-start(f32[64,1,1600]{2,1,0:T(1,128)} %reshape.355), calls=%async_computation | async-start | bytes 851968 | tf_op jit(solution)/shard_map/all_to_all | solution.py:106
  209.2 21.9 %all-to-all-start.1 = ((f32[64,1,1600]{2,1,0:T(1,128)}), f32[64,1,1600]{2,1,0:T(1,128)S(1)}, u32[]{:S(2)}, u32[]{:S(2)}) async-start(f32[64,1,1600]{2,1,0:T(1,128)} %reshape.357), calls=%async_computation.1 | async-start | bytes 851968 | tf_op jit(solution)/shard_map/all_to_all | solution.py:108
  219.9 387.4 %all-reduce.13.cloned.1.call-start = ((), (), s32[]{:S(2)}) async-start(), calls=%async_computation.2 | async-start | bytes 6627328 | tf_op jit(solution)/shard_map/psum | solution.py:154
  267.0 11.0 %copy-start.9 = (f32[64,2,320]{2,0,1:T(8,128)S(1)}, f32[64,2,320]{2,0,1:T(8,128)}, u32[]{:S(2)}) copy-start(f32[64,2,320]{2,0,1:T(8,128)} %copy-done.8) | copy-start | bytes 491524
  267.0 6.8 %collective-permute-start.1 = (bf16[20,1,2,320]{3,0,2,1:T(8,128)(2,1)S(1)}, bf16[20,1,2,320]{3,0,2,1:T(8,128)(2,1)S(1)}, u32[]{:S(2)}, u32[]{:S(2)}) collective-permute-start(bf16[20,1,2,320]{3,0,2,1:T(8,128)(2,1)S(1)} %fusion.234), channel_id=1, source_target_pairs={{1,0},{2,1},{3,2},{4,3},{5,4},{6,5},{7,6},{8,7},{9,8},{10,9},{11,1... | collective-permute-start | bytes 76808 | tf_op jit(solution)/shard_map/ppermute | solution.py:19
  270.5 5.9 collective-permute-start
  278.3 11.2 %collective-permute-start.11 = (bf16[64,1,2,320]{3,0,2,1:T(8,128)(2,1)S(1)}, bf16[64,1,2,320]{3,0,2,1:T(8,128)(2,1)S(1)}, u32[]{:S(2)}, u32[]{:S(2)}) collective-permute-start(bf16[64,1,2,320]{3,0,2,1:T(8,128)(2,1)S(1)} %bitcast.1356), channel_id=1, source_target_pairs={{1,0},{2,1},{3,2},{4,3},{5,4},{6,5},{7,6},{8,7},{9,8},{10,9},{11,1... | collective-permute-start | bytes 245768 | tf_op jit(solution)/shard_map/ppermute | solution.py:19
  281.7 7.9 %collective-permute-start.10 = (bf16[64,1,2,320]{3,0,2,1:T(8,128)(2,1)S(1)}, bf16[64,1,2,320]{3,0,2,1:T(8,128)(2,1)S(1)}, u32[]{:S(2)}, u32[]{:S(2)}) collective-permute-start(bf16[64,1,2,320]{3,0,2,1:T(8,128)(2,1)S(1)} %bitcast.1357), channel_id=1, source_target_pairs={{0,1},{1,2},{2,3},{3,4},{4,5},{5,6},{6,7},{7,8},{8,9},{9,10},{10,1... | collective-permute-start | bytes 245768 | tf_op jit(solution)/shard_map/ppermute | solution.py:16
  292.3 9.6 %collective-permute-start.13 = (bf16[64,1,2,320]{3,0,2,1:T(8,128)(2,1)S(1)}, bf16[64,1,2,320]{3,0,2,1:T(8,128)(2,1)S(1)}, u32[]{:S(2)}, u32[]{:S(2)}) collective-permute-start(bf16[64,1,2,320]{3,0,2,1:T(8,128)(2,1)S(1)} %bitcast.1359), channel_id=1, source_target_pairs={{1,0},{2,1},{3,2},{4,3},{5,4},{6,5},{7,6},{8,7},{9,8},{10,9},{11,1... | collective-permute-start | bytes 245768 | tf_op jit(solution)/shard_map/ppermute | solution.py:19
  295.7 6.6 %collective-permute-start.12 = (bf16[64,1,2,320]{3,0,2,1:T(8,128)(2,1)S(1)}, bf16[64,1,2,320]{3,0,2,1:T(8,128)(2,1)S(1)}, u32[]{:S(2)}, u32[]{:S(2)}) collective-permute-start(bf16[64,1,2,320]{3,0,2,1:T(8,128)(2,1)S(1)} %bitcast.1360), channel_id=1, source_target_pairs={{0,1},{1,2},{2,3},{3,4},{4,5},{5,6},{6,7},{7,8},{8,9},{9,10},{10,1... | collective-permute-start | bytes 245768 | tf_op jit(solution)/shard_map/ppermute | solution.py:16
  305.1 9.9 %collective-permute-start.15 = (bf16[64,1,2,320]{3,0,2,1:T(8,128)(2,1)S(1)}, bf16[64,1,2,320]{3,0,2,1:T(8,128)(2,1)S(1)}, u32[]{:S(2)}, u32[]{:S(2)}) collective-permute-start(bf16[64,1,2,320]{3,0,2,1:T(8,128)(2,1)S(1)} %bitcast.1362), channel_id=1, source_target_pairs={{1,0},{2,1},{3,2},{4,3},{5,4},{6,5},{7,6},{8,7},{9,8},{10,9},{11,1... | collective-permute-start | bytes 245768 | tf_op jit(solution)/shard_map/ppermute | solution.py:19
  307.1 8.2 %collective-permute-start.14 = (bf16[64,1,2,320]{3,0,2,1:T(8,128)(2,1)S(1)}, bf16[64,1,2,320]{3,0,2,1:T(8,128)(2,1)S(1)}, u32[]{:S(2)}, u32[]{:S(2)}) collective-permute-start(bf16[64,1,2,320]{3,0,2,1:T(8,128)(2,1)S(1)} %bitcast.1363), channel_id=1, source_target_pairs={{0,1},{1,2},{2,3},{3,4},{4,5},{5,6},{6,7},{7,8},{8,9},{9,10},{10,1... | collective-permute-start | bytes 245768 | tf_op jit(solution)/shard_map/ppermute | solution.py:16
  318.1 9.5 %collective-permute-start.17 = (bf16[64,1,2,320]{3,0,2,1:T(8,128)(2,1)S(1)}, bf16[64,1,2,320]{3,0,2,1:T(8,128)(2,1)S(1)}, u32[]{:S(2)}, u32[]{:S(2)}) collective-permute-start(bf16[64,1,2,320]{3,0,2,1:T(8,128)(2,1)S(1)} %bitcast.1353), channel_id=1, source_target_pairs={{1,0},{2,1},{3,2},{4,3},{5,4},{6,5},{7,6},{8,7},{9,8},{10,9},{11,1... | collective-permute-start | bytes 245768 | tf_op jit(solution)/shard_map/ppermute | solution.py:19
  320.0 8.6 %collective-permute-start.16 = (bf16[64,1,2,320]{3,0,2,1:T(8,128)(2,1)S(1)}, bf16[64,1,2,320]{3,0,2,1:T(8,128)(2,1)S(1)}, u32[]{:S(2)}, u32[]{:S(2)}) collective-permute-start(bf16[64,1,2,320]{3,0,2,1:T(8,128)(2,1)S(1)} %bitcast.1354), channel_id=1, source_target_pairs={{0,1},{1,2},{2,3},{3,4},{4,5},{5,6},{6,7},{7,8},{8,9},{9,10},{10,1... | collective-permute-start | bytes 245768 | tf_op jit(solution)/shard_map/ppermute | solution.py:16
  (17 other events, 89.2 us)
Sparse Core Ops, SparseCore 0:
  327.8 279.5 all-reduce.12
where the time goes:
time: 632 us; the launch traced here: 623 us
  waiting for transfers between devices  288 us (46%)
  local copies, waits for them, and re-layouts  127 us (20%)
  starting transfers between devices  108 us (17%)
  matrix products  72.3 us (11%)
  between operations  16.6 us (3%)
  other arithmetic  11.8 us (2%)
    psum x1, waiting for transfers between devices, body(): lax.psum((local_tuple[0], local_tuple[1], local_tuple[2], local_tuple[3],...  275 us
    unnamed x315, local copies, waits for them, and re-layouts  71.1 us
    ppermute x10, starting transfers between devices, padded_2(): lax.ppermute(lax.slice_in_dim(block, block.shape[dim] - width, None, axis...  47.1 us
    ppermute x10, starting transfers between devices, padded_2(): lax.ppermute(lax.slice_in_dim(block, 0, width, axis=dim), axis, backward)  26.3 us
    all_to_all x1, starting transfers between devices, normal_operator(): lax.all_to_all(spectra, 'slab', split_axis=4, concat_axis=5, tiled=True)  23.7 us
  transfers between devices with their start and end apart: 23, of which 6 were waited for; matrix products, arithmetic and copies ran while one was open for 10% of the time, Pallas kernels for 0%

commit v1 on v0

--- a/solution.py
+++ b/solution.py
@@ -6,6 +6,12 @@
 
 ETA_STEP = 0.5
 PRECISE = lax.Precision.HIGHEST
+
+
+def supply_the_boxes(group_axis, packet, device_axis):
+    for h in (group_axis, device_axis):
+        packet = lax.psum(packet, h)
+    return packet
 
 
 def padded_2(block, sides, width):
@@ -151,9 +157,10 @@
             delta_grad = (back_grad * silu_slope(pre_acts[level - 1])).astype(jnp.bfloat16)
     image_grads = [direct + back_grad]
     local_tuple = (local_sums[0], local_sums[1], local_sums[2], local_sums[3], local_sums[4])
-    summed = lax.psum(
+    summed = supply_the_boxes(
+        "subj",
         (local_tuple[0], local_tuple[1], local_tuple[2], local_tuple[3], local_tuple[4]),
-        ("subj", "slab"),
+        "slab",
     )
     total_cells = (
         image.shape[0]

time: 632 us -> 1220 us (1.93)
  waiting for transfers between devices: 288 us -> 857 us
  local copies, waits for them, and re-layouts: 127 us -> 144 us
    psum x1 -> x2, waiting for transfers between devices: 275 us -> 844 us  [supply_the_boxes(): packet = lax.psum(packet, h)]
    unnamed x315, local copies, waits for them, and re-layouts: 71.1 us -> 87.5 us
  transfers between devices with their start and end apart: 23 -> 24, of which waited for: 6 -> 7; matrix products, arithmetic and copies ran while one was open for 10% -> 7% of each run, Pallas kernels for 0% -> 0%
where the time goes in v1:
time: 1220 us; the launch traced here: 1210 us
  waiting for transfers between devices  857 us (70%)
  local copies, waits for them, and re-layouts  144 us (12%)
  starting transfers between devices  108 us (9%)
  matrix products  74 us (6%)
  between operations  16.4 us (1%)
    psum x2, waiting for transfers between devices, supply_the_boxes(): packet = lax.psum(packet, h)  844 us
    unnamed x315, local copies, waits for them, and re-layouts  87.5 us
    ppermute x10, starting transfers between devices, padded_2(): lax.ppermute(lax.slice_in_dim(block, block.shape[dim] - width, None, axis...  47.1 us
    ppermute x10, starting transfers between devices, padded_2(): lax.ppermute(lax.slice_in_dim(block, 0, width, axis=dim), axis, backward)  26.3 us
  transfers between devices with their start and end apart: 24, of which 7 were waited for; matrix products, arithmetic and copies ran while one was open for 7% of the time, Pallas kernels for 0%

profile of v1, /device:TPU:4, one launch (start us, length us, event | category | flops | bytes accessed | tf_op | source)
XLA Modules:
  0.0 1210.9 jit_solution(384143983951208783)
XLA Ops:
  9.8 3.4 collective-permute-start.2
  24.2 4.4 collective-permute-start.4
  34.4 3.1 collective-permute-start.7
  37.5 5.0 collective-permute-start.6
  50.2 6.0 collective-permute-start.8
  65.4 6.2 collective-permute-start.18
  71.7 5.0 copy.3471
  76.7 8.8 reshape.355
  85.5 23.7 %all-to-all-start = ((f32[64,1,1600]{2,1,0:T(1,128)}), f32[64,1,1600]{2,1,0:T(1,128)S(1)}, u32[]{:S(2)}, u32[]{:S(2)}) async-start(f32[64,1,1600]{2,1,0:T(1,128)} %reshape.355), calls=%async_computation | async-start | bytes 851968 | tf_op jit(solution)/shard_map/all_to_all | solution.py:112
  109.2 4.1 copy.3476
  131.0 9.9 reshape.356
  156.2 3.1 copy.3478
  159.3 12.0 convolution_bitcast_fusion
  176.8 3.1 copy.3475
  179.9 11.6 convolution_bitcast_fusion.1
  196.6 5.9 copy.3483
  202.5 6.7 reshape.357
  209.2 10.7 all-to-all-start.1
  222.8 8.3 all-to-all-done.1
  232.8 7.4 reshape.358
  240.2 2.8 bitcast_bitcast_fusion
  252.0 3.4 copy.3486
  263.7 3.3 add_reduce_fusion
  267.1 3.5 collective-permute-start.1
  278.3 3.4 collective-permute-start.11
  286.0 3.6 fusion.37
  292.4 3.4 collective-permute-start.13
  295.7 4.4 collective-permute-start.12
  307.1 6.2 collective-permute-start.14
  320.1 6.4 collective-permute-start.16
  343.6 124.7 %all-reduce.17.cloned.1.call-done = (f32[27,64,20]{1,0,2:T(8,128)}, f32[27,64,64]{1,2,0:T(8,128)}, f32[27,64,64]{1,2,0:T(8,128)}, f32[27,64,64]{1,2,0:T(8,128)}, f32[27,20,64]{2,1,0:T(8,128)}) async-done(((f32[27,64,20]{1,0,2:T(8,128)}, f32[27,64,64]{1,2,0:T(8,128)}, f32[27,64,64]{1,2,0:T(8,128)}, f32[27,64,64]{1,2,0:T(8,128)}, f32[27,20,64]{2,1,0:T(8,128)}), (f32[27,64,20]{1,0,2:T(8,128)}, ...) | async-done | bytes 1603600 | tf_op jit(solution)/shard_map/psum | solution.py:13
  475.4 719.5 %all-reduce.15.cloned.1.call-done = (f32[27,64,20]{1,0,2:T(8,128)}, f32[27,64,64]{1,2,0:T(8,128)}, f32[27,64,64]{1,2,0:T(8,128)}, f32[27,64,64]{1,2,0:T(8,128)}, f32[27,20,64]{2,1,0:T(8,128)}) async-done(((f32[27,64,20]{1,0,2:T(8,128)}, f32[27,64,64]{1,2,0:T(8,128)}, f32[27,64,64]{1,2,0:T(8,128)}, f32[27,64,64]{1,2,0:T(8,128)}, f32[27,20,64]{2,1,0:T(8,128)}), (f32[27,64,20]{1,0,2:T(8,128)}, ...) | async-done | bytes 1603600 | tf_op jit(solution)/shard_map/psum | solution.py:13
  (430 shorter events, 161.3 us)
Async XLA Ops:
  7.2 54.1 %copy-start = (bf16[3,3,3,64,64]{4,3,2,1,0:T(8,128)(2,1)S(1)}, bf16[3,3,3,64,64]{4,3,2,1,0:T(8,128)(2,1)}, u32[]{:S(2)}) copy-start(bf16[3,3,3,64,64]{4,3,2,1,0:T(8,128)(2,1)} %param.16) | copy-start | bytes 663556
  7.2 12.6 %copy-start.24 = (bf16[1,20,1,2,320]{4,3,2,1,0:T(2,128)(2,1)S(1)}, bf16[1,20,1,2,320]{4,3,2,1,0:T(2,128)(2,1)}, u32[]{:S(2)}) copy-start(bf16[1,20,1,2,320]{4,3,2,1,0:T(2,128)(2,1)} %param.9) | copy-start | bytes 76804
  7.2 13.9 %copy-start.22 = (bf16[3,3,3,64,20]{3,4,2,1,0:T(8,128)(2,1)S(1)}, bf16[3,3,3,64,20]{3,4,2,1,0:T(8,128)(2,1)}, u32[]{:S(2)}) copy-start(bf16[3,3,3,64,20]{3,4,2,1,0:T(8,128)(2,1)} %param.13) | copy-start | bytes 207364
  7.2 10.4 collective-permute-start.3
  9.8 7.8 collective-permute-start.2
  21.5 10.0 collective-permute-start.5
  24.2 7.3 collective-permute-start.4
  33.7 11.6 copy-start.1
  34.4 11.0 collective-permute-start.7
  37.5 7.8 collective-permute-start.6
  47.6 11.5 copy-start.3
  48.3 10.8 collective-permute-start.9
  50.2 8.9 collective-permute-start.8
  63.4 59.2 %copy-start.8 = (f32[64,2,320]{2,0,1:T(8,128)}, f32[64,2,320]{2,0,1:T(8,128)S(1)}, u32[]{:S(2)}) copy-start(f32[64,2,320]{2,0,1:T(8,128)S(1)} %fusion.49) | copy-start | bytes 491524
  63.4 49.9 %collective-permute-start.19 = (bf16[64,1,2,320]{3,0,2,1:T(8,128)(2,1)S(1)}, bf16[64,1,2,320]{3,0,2,1:T(8,128)(2,1)S(1)}, u32[]{:S(2)}, u32[]{:S(2)}) collective-permute-start(bf16[64,1,2,320]{3,0,2,1:T(8,128)(2,1)S(1)} %fusion.346), channel_id=1, source_target_pairs={{1,0},{2,1},{3,2},{4,3},{5,4},{6,5},{7,6},{8,7},{9,8},{10,9},{11,1... | collective-permute-start | bytes 245768 | tf_op jit(solution)/shard_map/ppermute | solution.py:25
  65.4 48.0 %collective-permute-start.18 = (bf16[64,1,2,320]{3,0,2,1:T(8,128)(2,1)S(1)}, bf16[64,1,2,320]{3,0,2,1:T(8,128)(2,1)S(1)}, u32[]{:S(2)}, u32[]{:S(2)}) collective-permute-start(bf16[64,1,2,320]{3,0,2,1:T(8,128)(2,1)S(1)} %fusion.346), channel_id=1, source_target_pairs={{0,1},{1,2},{2,3},{3,4},{4,5},{5,6},{6,7},{7,8},{8,9},{9,10},{10,1... | collective-permute-start | bytes 245768 | tf_op jit(solution)/shard_map/ppermute | solution.py:22
  76.7 32.5 %copy-start.16 = (f32[10,10,64,2,5]{2,3,4,1,0:T(2,128)S(1)}, f32[10,10,64,2,5]{2,3,4,1,0:T(2,128)}, u32[]{:S(2)}) copy-start(f32[10,10,64,2,5]{2,3,4,1,0:T(2,128)} %param.12) | copy-start | bytes 768004
  85.5 43.4 %all-to-all-start = ((f32[64,1,1600]{2,1,0:T(1,128)}), f32[64,1,1600]{2,1,0:T(1,128)S(1)}, u32[]{:S(2)}, u32[]{:S(2)}) async-start(f32[64,1,1600]{2,1,0:T(1,128)} %reshape.355), calls=%async_computation | async-start | bytes 851968 | tf_op jit(solution)/shard_map/all_to_all | solution.py:112
  209.2 21.9 %all-to-all-start.1 = ((f32[64,1,1600]{2,1,0:T(1,128)}), f32[64,1,1600]{2,1,0:T(1,128)S(1)}, u32[]{:S(2)}, u32[]{:S(2)}) async-start(f32[64,1,1600]{2,1,0:T(1,128)} %reshape.357), calls=%async_computation.1 | async-start | bytes 851968 | tf_op jit(solution)/shard_map/all_to_all | solution.py:114
  220.0 248.3 %all-reduce.17.cloned.1.call-start = ((), (), s32[]{:S(2)}) async-start(), calls=%async_computation.3 | async-start | bytes 6627328 | tf_op jit(solution)/shard_map/psum | solution.py:13
  267.1 6.8 collective-permute-start.1
  270.6 5.9 collective-permute-start
  278.3 11.2 collective-permute-start.11
  281.7 7.9 collective-permute-start.10
  292.4 9.6 collective-permute-start.13
  295.7 6.6 collective-permute-start.12
  305.2 9.9 collective-permute-start.15
  307.1 8.2 collective-permute-start.14
  318.2 9.6 collective-permute-start.17
  320.1 8.6 collective-permute-start.16
  327.7 867.2 %all-reduce.15.cloned.1.call-start = ((), (), s32[]{:S(2)}) async-start(), calls=%async_computation.2 | async-start | bytes 6627328 | tf_op jit(solution)/shard_map/psum | solution.py:13
  340.8 131.7 %copy-start.23 = (bf16[3,3,3,64,20]{3,4,2,1,0:T(8,128)(2,1)S(1)}, bf16[3,3,3,64,20]{3,4,2,1,0:T(8,128)(2,1)}, u32[]{:S(2)}) copy-start(bf16[3,3,3,64,20]{3,4,2,1,0:T(8,128)(2,1)} %param.13) | copy-start | bytes 207364
  (18 other events, 109.3 us)
Sparse Core Ops, SparseCore 0:
  327.8 140.4 all-reduce.16
  471.6 723.2 all-reduce.14
